TPU v7x, 32 devices: a whole 2x2x4 slice. The times are simulated.
32 devices in a mesh: grp: 2 (over x), tm: 16 (over z, y, core).
Axes of the slice: x: 2, y: 2, z: 4, core: 2. Of those that a mesh axis runs over, the one named last changes fastest.
Arguments:
- transformer_tiles: float32 [6144, 128], P(('grp', 'tm')), parts along dimension 0, may hold values from -6 to 6
- global_tile_index: int32 [32, 192], P(('grp', 'tm')), parts along dimension 0, may hold values from 0 to 3071, as said below
- video_frame_count: int32 [16], P('grp'), parts along dimension 0, may hold values from 1 to 16, 64 in all
- input_conv_weight: float32 [3, 144, 384], replicated, may hold values from -0.3125 to 0.3125
- input_conv_bias: float32 [384], replicated, may hold values from -3 to 3
- first_norm_gain: float32 [384], replicated, may hold values from 0.1 to 1.9
- residual_conv_weight: bfloat16 [3, 3456, 384], replicated, may hold values from -0.0625 to 0.0625
- residual_conv_bias: float32 [384], replicated, may hold values from -3 to 3
- second_norm_gain: float32 [384], replicated, may hold values from 0.1 to 1.9
Outputs:
- block_input: bfloat16 [128, 16, 24, 384], P(('grp', 'tm')), parts along dimension 0
- branch_act: bfloat16 [128, 16, 24, 384], P(('grp', 'tm')), parts along dimension 0
There are 2 independent parts, one for each index of `grp`. A program takes and returns all parts, laid end to end along the dimension named above; an argument that names none is the same for every part. Nothing has to cross between parts.
Inputs may be any that keep to these rules, and one draw needn't show every extreme that they name: `global_tile_index`: entry (j, i) is the id receiver * 192 + slot of the i-th tile that DiT owner j stores; every id of 0 to 3071 appears exactly once; an owner holds at most 24 tiles of any one receiver, and in every draw some owners hold exactly 24 of one receiver. Slot s of receiver r is latent frame r * 4 + s // 48, row (s // 3) % 16, columns 8 (s % 3) onward. `video_frame_count`: the counts sum to 64; the longest video has exactly 16 frames.
All inputs are finite; a program needn't handle non-finite values.
Results may differ from a plain program's by a relative error of at most 0.0054.
Values may be sent and summed in bfloat16 or wider, within the bound.
A program may use at most 64 MiB of HBM per device.

v0:
```python
import functools

import jax
import jax.numpy as jnp
from jax import lax
from jax.experimental import pallas as pl
from jax.experimental.pallas import tpu as pltpu
from jax.sharding import PartitionSpec as P

LT = 4
HL = 16
WL = 24
MESH = pl.DeviceIdType.MESH
F32 = jnp.float32
BF16 = jnp.bfloat16


def iota(shape, dim):
    return lax.broadcasted_iota(jnp.int32, shape, dim)


def regroup_kernel(n, br, tiles_ref, ids_ref, win_ref, out_buf, in_buf, own_buf, halo_buf,
                   send_sem, recv_sem, halo_sems):
    count = tiles_ref.shape[0]
    me = lax.axis_index("tm")
    barrier = pltpu.get_barrier_semaphore()

    def greet(k, carry):
        pl.semaphore_signal(barrier, inc=1, device_id={"tm": lax.rem(me + k, n)}, device_id_type=MESH)
        return carry

    lax.fori_loop(1, n, greet, 0)

    ids = ids_ref[...].astype(F32)
    target = jnp.floor((ids + 0.5) * (1.0 / count))
    slot = ids - target * count
    rows, cols = iota((count, count), 0), iota((count, count), 1)
    target_col = jnp.sum(jnp.where(rows == cols, target, 0.0), axis=1, keepdims=True)
    same = (target_col == target) & (rows < cols)
    rank = jnp.sum(jnp.where(same, 1.0, 0.0), axis=0, keepdims=True)
    rank_col = jnp.sum(jnp.where(rows == cols, rank, 0.0), axis=1, keepdims=True)
    position = target * br + rank
    total = n * br
    spread = jnp.where(iota((total, count), 0).astype(F32) == position, 1.0, 0.0).astype(BF16)
    slots_at = jnp.where(iota((n, count), 0).astype(F32) == target, slot + 1.0, 0.0).astype(BF16)
    lanes_at = jnp.where((iota((count, 128), 1) % br).astype(F32) == rank_col, 1.0, 0.0).astype(BF16)
    slot_rows = jnp.dot(slots_at, lanes_at, preferred_element_type=F32).astype(BF16)
    last = jnp.where(iota((total, n), 0) == iota((total, n), 1) * br + br - 1, 1.0, 0.0).astype(BF16)
    outbound = jnp.dot(spread, tiles_ref[...].astype(BF16), preferred_element_type=F32)
    outbound = outbound + jnp.dot(last, slot_rows, preferred_element_type=F32)
    out_buf[...] = outbound.astype(BF16).reshape(n, br, 128)

    pl.semaphore_wait(barrier, n - 1)

    def block_copy(k):
        peer = lax.rem(me + k, n)
        return pltpu.make_async_remote_copy(
            src_ref=out_buf.at[peer], dst_ref=in_buf.at[me], send_sem=send_sem.at[k],
            recv_sem=recv_sem.at[k], device_id={"tm": peer}, device_id_type=MESH)

    def start(k, carry):
        block_copy(k).start()
        return carry

    def finish(k, carry):
        block_copy(k).wait()
        return carry

    lax.fori_loop(1, n, start, 0)
    in_buf[me] = out_buf[me]
    lax.fori_loop(1, n, finish, 0)

    incoming = in_buf[...].reshape(total, 128)
    pick = jnp.where(iota((n, total), 1) == iota((n, total), 0) * br + br - 1, 1.0, 0.0).astype(BF16)
    in_slots = jnp.dot(pick, incoming, preferred_element_type=F32)
    per_tile = 128 // br
    pieces = []
    for k in range(total // 128):
        own = iota((n, 128), 0) == k * per_tile + iota((n, 128), 1) // br
        slot_row = jnp.sum(jnp.where(own, in_slots, 0.0), axis=0, keepdims=True)
        hit = iota((count, 128), 0).astype(F32) + 1.0 == slot_row
        pieces.append(jnp.where(hit, 1.0, 0.0).astype(BF16))
    gather = jnp.concatenate(pieces, axis=1)
    own_buf[...] = jnp.dot(gather, incoming, preferred_element_type=F32).astype(BF16)
    halo = pltpu.make_async_remote_copy(
        src_ref=own_buf, dst_ref=halo_buf, send_sem=halo_sems.at[0], recv_sem=halo_sems.at[1],
        device_id={"tm": lax.rem(me + 1, n)}, device_id_type=MESH)
    halo.start()
    win_ref[count:] = own_buf[...]
    halo.wait()
    win_ref[:count] = halo_buf[...]


def silu_norm(values, gain):
    normed = values * lax.rsqrt(jnp.mean(values * values, axis=-1, keepdims=True) + 1e-06)
    scaled = normed * gain
    return scaled / (1.0 + jnp.exp(-scaled))


def decode_kernel(win_ref, count_ref, w_in_ref, b_in_ref, g_one_ref, w_res_ref, b_res_ref, g_two_ref,
                  block_ref, branch_ref, w_buf, lat, lhs, edge, toep, pre, acts, acc, masks, sems):
    c = b_in_ref.shape[1]
    frame = HL * WL
    per_frame = frame // 8
    stride = per_frame + 8
    copies = [
        pltpu.make_async_copy(
            w_res_ref.at[d, pl.ds(a * 3 * c, 3 * c), :], w_buf.at[d, :, pl.ds(a * c, c)], sems.at[d * 3 + a])
        for d in range(3) for a in range(3)
    ]
    for copy in copies:
        copy.start()

    first = lax.axis_index("tm") * LT - 2
    for g in range(LT + 2):
        begin = jnp.int32(0)
        bound = jnp.int32(0)
        for v in range(count_ref.shape[0]):
            begin = jnp.where(bound <= first + g, bound, begin)
            bound = bound + count_ref[v]
        masks[0, g] = 1.0
        masks[1, g] = jnp.where(first + g - 1 >= begin, 1.0, 0.0)
        masks[2, g] = jnp.where(first + g - 2 >= begin, 1.0, 0.0)

    toep[...] = jnp.zeros_like(toep)
    for d in range(3):
        for a in range(3):
            j = 128 * (3 * d + a)
            taps = w_in_ref[d, 48 * a:48 * a + 48, :].astype(BF16)
            for x in range(8):
                low, high = max(0, x - 1), min(7, x + 1)
                skip = 16 * (low - x + 1)
                toep[j + 16 * low:j + 16 * high + 16, c * x:c * x + c] = taps[skip:skip + 16 * (high - low + 1)]
            toep[j + 112:j + 128, 8 * c:9 * c] = taps[:16]
            toep[j:j + 16, 9 * c:10 * c] = taps[32:]

    lat[...] = jnp.zeros_like(lat)
    for g in range(LT + 4):
        lat[stride * g + 3:stride * g + 3 + per_frame, :] = win_ref[per_frame * g:per_frame * (g + 1), :].astype(F32)
    row, lane = iota((per_frame, 128), 0) % 3, iota((per_frame, 128), 1)
    from_right = (lane < 16) & (row != 2)
    from_left = (lane >= 112) & (row != 0)
    for g in range(LT + 2):
        for d in range(3):
            for a in range(3):
                j = 128 * (3 * d + a)
                base = stride * (g + 2 - d) + 3 * a
                piece = lat[base:base + per_frame, :] * masks[d, g]
                lhs[per_frame * g:per_frame * (g + 1), j:j + 128] = piece.astype(BF16)
                beside = jnp.where(from_right, pltpu.roll(piece, per_frame - 1, 0),
                                   jnp.where(from_left, pltpu.roll(piece, 1, 0), 0.0))
                edge[per_frame * g:per_frame * (g + 1), j:j + 128] = beside.astype(BF16)

    rows = per_frame * (LT + 2)
    sides = jnp.dot(edge[...], toep[:, 8 * c:], preferred_element_type=F32)
    for p in range(4):
        out = jnp.dot(lhs[...], toep[:, 2 * c * p:2 * c * (p + 1)], preferred_element_type=F32)
        even, odd = out[:, :c], out[:, c:]
        if p == 0:
            even = even + sides[:, :c]
        if p == 3:
            odd = odd + sides[:, c:]
        for e, part in enumerate((even, odd)):
            for q in range(c // 128):
                pre[q, pl.ds(2 * p + e, rows, stride=8), :] = part[:, 128 * q:128 * q + 128]

    column = iota((frame, c), 0) % WL

    def act_frame(g, carry):
        at = pl.ds(pl.multiple_of(g * frame, frame), frame)
        rounded = (jnp.concatenate([pre[q, at, :] for q in range(c // 128)], axis=1) + b_in_ref[...]).astype(BF16)

        @pl.when(g >= 2)
        def _():
            block_ref[g - 2] = rounded

        act = silu_norm(rounded.astype(F32), g_one_ref[...])
        acts[at, :c] = jnp.where(column == 0, 0.0, pltpu.roll(act, 1, 0)).astype(BF16)
        acts[at, c:2 * c] = act.astype(BF16)
        acts[at, 2 * c:] = jnp.where(column == WL - 1, 0.0, pltpu.roll(act, frame - 1, 0)).astype(BF16)
        return carry

    lax.fori_loop(0, LT + 2, act_frame, 0)

    acc[...] = jnp.zeros_like(acc)
    for copy in copies:
        copy.wait()

    def product(i, carry):
        d, f = i // LT, i % LT
        at = pl.ds(pl.multiple_of((f + 2 - d) * frame, frame), frame)
        out = jnp.dot(acts[at, :], w_buf[d], preferred_element_type=F32) * masks[d, f + 2]
        for a in range(3):
            acc[f, WL * (2 - a):WL * (2 - a) + frame, :] += out[:, c * a:c * a + c]
        return carry

    lax.fori_loop(0, 3 * LT, product, 0)

    def last_frame(f, carry):
        branch_ref[f] = silu_norm(acc[f, WL:WL + frame, :] + b_res_ref[...], g_two_ref[...]).astype(BF16)
        return carry

    lax.fori_loop(0, LT, last_frame, 0)


def local(
    transformer_tiles,
    global_tile_index,
    video_frame_count,
    input_conv_weight,
    input_conv_bias,
    first_norm_gain,
    residual_conv_weight,
    residual_conv_bias,
    second_norm_gain,
):
    n = lax.axis_size("tm")
    count = transformer_tiles.shape[0]
    c = input_conv_bias.shape[0]
    cap = max(2, 2 * count // n)
    br = 16 * ((cap + 16) // 16)
    vmem = pl.BlockSpec(memory_space=pltpu.VMEM)
    window = pl.pallas_call(
        functools.partial(regroup_kernel, n, br),
        out_shape=jax.ShapeDtypeStruct((2 * count, 128), BF16),
        in_specs=[vmem, vmem],
        out_specs=vmem,
        scratch_shapes=[
            pltpu.VMEM((n, br, 128), BF16),
            pltpu.VMEM((n, br, 128), BF16),
            pltpu.VMEM((count, 128), BF16),
            pltpu.VMEM((count, 128), BF16),
            pltpu.SemaphoreType.DMA((n,)),
            pltpu.SemaphoreType.DMA((n,)),
            pltpu.SemaphoreType.DMA((2,)),
        ],
        compiler_params=pltpu.CompilerParams(
            collective_id=0, has_side_effects=True, vmem_limit_bytes=32 * 1024 * 1024),
    )(transformer_tiles, global_tile_index)

    frame = HL * WL
    act_rows = (LT + 2) * frame
    block_input, branch_act = pl.pallas_call(
        decode_kernel,
        out_shape=[jax.ShapeDtypeStruct((LT, frame, c), BF16)] * 2,
        in_specs=[vmem, pl.BlockSpec(memory_space=pltpu.SMEM), vmem, vmem, vmem,
                  pl.BlockSpec(memory_space=pl.ANY), vmem, vmem],
        out_specs=[vmem, vmem],
        scratch_shapes=[
            pltpu.VMEM((3, 3 * c, 3 * c), BF16),
            pltpu.VMEM(((LT + 4) * (frame // 8 + 8), 128), F32),
            pltpu.VMEM((act_rows // 8, 9 * 128), BF16),
            pltpu.VMEM((act_rows // 8, 9 * 128), BF16),
            pltpu.VMEM((9 * 128, 10 * c), BF16),
            pltpu.VMEM((c // 128, act_rows, 128), F32),
            pltpu.VMEM((act_rows, 3 * c), BF16),
            pltpu.VMEM((LT, frame + 2 * WL, c), F32),
            pltpu.SMEM((3, LT + 2), F32),
            pltpu.SemaphoreType.DMA((9,)),
        ],
        compiler_params=pltpu.CompilerParams(vmem_limit_bytes=58 * 1024 * 1024),
        cost_estimate=pl.CostEstimate(flops=16_000_000_000, bytes_accessed=12_000_000, transcendentals=2_000_000),
    )(window, video_frame_count, input_conv_weight, input_conv_bias[None], first_norm_gain[None],
      residual_conv_weight, residual_conv_bias[None], second_norm_gain[None])
    return (block_input.reshape(LT, HL, WL, c), branch_act.reshape(LT, HL, WL, c))


def solution(mesh):
    placed = (
        P(("grp", "tm"), None),
        P(("grp", "tm"), None),
        P("grp"),
        P(),
        P(),
        P(),
        P(),
        P(),
        P(),
    )
    return jax.shard_map(
        local,
        mesh=mesh,
        in_specs=placed,
        out_specs=(P(("grp", "tm"), None, None, None), P(("grp", "tm"), None, None, None)),
        check_vma=False,
    )
```

profile of v0, /device:TPU:0, one launch (start us, length us, event | category | flops | bytes accessed | tf_op | source)
XLA Modules:
  0.0 51.7 jit_solution(15807120708273707128)
XLA Ops:
  0.6 1.2 %broadcast_in_dim.12.b_in_ref = f32[1,384]{1,0:T(1,128)} reshape(f32[384]{0:T(512)} %param.13) | data formatting | bytes 3072 | tf_op jit(solution)/shard_map/broadcast_in_dim | solution.py:263
  1.9 1.3 %broadcast_in_dim.13.g_one_ref = f32[1,384]{1,0:T(1,128)} reshape(f32[384]{0:T(512)} %param.14) | data formatting | bytes 3072 | tf_op jit(solution)/shard_map/broadcast_in_dim | solution.py:263
  3.1 1.3 %broadcast_in_dim.14.b_res_ref = f32[1,384]{1,0:T(1,128)} reshape(f32[384]{0:T(512)} %param.16) | data formatting | bytes 3072 | tf_op jit(solution)/shard_map/broadcast_in_dim | solution.py:264
  4.4 1.2 %broadcast_in_dim.15.g_two_ref = f32[1,384]{1,0:T(1,128)} reshape(f32[384]{0:T(512)} %param.17) | data formatting | bytes 3072 | tf_op jit(solution)/shard_map/broadcast_in_dim | solution.py:264
  5.6 0.0 copy-start
  5.6 0.9 %copy-done = f32[192,128]{1,0:T(8,128)S(1)} copy-done((f32[192,128]{1,0:T(8,128)S(1)}, f32[192,128]{1,0:T(8,128)}, u32[]{:S(2)}) %copy-start) | copy-done | bytes 98328
  6.5 0.0 copy-start.2
  6.5 0.7 %copy-done.2 = s32[1,192]{1,0:T(1,128)S(1)} copy-done((s32[1,192]{1,0:T(1,128)S(1)}, s32[1,192]{1,0:T(1,128)}, u32[]{:S(2)}) %copy-start.2) | copy-done | bytes 792
  7.2 15.9 %shard_map.104.win_ref = bf16[384,128]{1,0:T(8,128)(2,1)S(1)} custom-call(f32[192,128]{1,0:T(8,128)S(1)} %copy-done, s32[1,192]{1,0:T(1,128)S(1)} %copy-done.2), custom_call_target="tpu_custom_call" | custom-call | tf_op jit(solution)/shard_map/pallas_call | solution.py:223
  23.1 0.0 copy-start.1
  23.1 0.6 %copy-done.1 = bf16[384,128]{1,0:T(8,128)(2,1)} copy-done((bf16[384,128]{1,0:T(8,128)(2,1)}, bf16[384,128]{1,0:T(8,128)(2,1)S(1)}, u32[]{:S(2)}) %copy-start.1) | copy-done | bytes 98328
  23.8 27.9 %shard_map.105 = (bf16[4,384,384]{2,1,0:T(8,128)(2,1)}, bf16[4,384,384]{2,1,0:T(8,128)(2,1)}) custom-call(bf16[384,128]{1,0:T(8,128)(2,1)} %copy-done.1, s32[8]{0:T(128)} %count_ref.1, f32[3,144,384]{2,1,0:T(8,128)} %w_in_ref.1, f32[1,384]{1,0:T(1,128)} %broadcast_in_dim.12.b_in_ref, f32[1,384]{1,0:T(1,128)} %broadcast_in_dim.13.g_one_ref, ...), custom_call_target="tpu_custom_call" | custom-call | flops 16000000000 | bytes 12000000 | tf_op jit(solution)/shard_map/pallas_call | solution.py:243
Async XLA Ops:
  5.6 0.9 %copy-start = (f32[192,128]{1,0:T(8,128)S(1)}, f32[192,128]{1,0:T(8,128)}, u32[]{:S(2)}) copy-start(f32[192,128]{1,0:T(8,128)} %tiles_ref.1) | copy-start | bytes 294916
  6.5 0.7 %copy-start.2 = (s32[1,192]{1,0:T(1,128)S(1)}, s32[1,192]{1,0:T(1,128)}, u32[]{:S(2)}) copy-start(s32[1,192]{1,0:T(1,128)} %ids_ref.1) | copy-start | bytes 2308
  23.1 0.6 %copy-start.1 = (bf16[384,128]{1,0:T(8,128)(2,1)}, bf16[384,128]{1,0:T(8,128)(2,1)S(1)}, u32[]{:S(2)}) copy-start(bf16[384,128]{1,0:T(8,128)(2,1)S(1)} %shard_map.104.win_ref) | copy-start | bytes 294916
where the time goes:
time: 51.9 us; the launch traced here: 51.7 us
  Pallas kernels  43.8 us (84%)
  local copies, waits for them, and re-layouts  7.19 us (14%)
  between operations  0.65 us (1%)
    pallas_call x1, Pallas kernels, local(): pl.pallas_call(decode_kernel, out_shape=[jax.ShapeDtypeStruct((LT, frame,...  27.9 us
    pallas_call x1, Pallas kernels, local(): pl.pallas_call(functools.partial(regroup_kernel, n, br), out_shape=jax.Sh...  15.9 us
    unnamed x6, local copies, waits for them, and re-layouts  2.19 us
    broadcast_in_dim x1, local copies, waits for them, and re-layouts, local(): first_norm_gain[None]  1.26 us
    broadcast_in_dim x1, local copies, waits for them, and re-layouts, local(): residual_conv_bias[None]  1.26 us
    broadcast_in_dim x1, local copies, waits for them, and re-layouts, local(): input_conv_bias[None]  1.24 us
    broadcast_in_dim x1, local copies, waits for them, and re-layouts, local(): second_norm_gain[None]  1.24 us

commit v1 on v0

--- a/solution.py
+++ b/solution.py
@@ -19,9 +19,13 @@
     return lax.broadcasted_iota(jnp.int32, shape, dim)
 
 
-def regroup_kernel(n, br, tiles_ref, ids_ref, win_ref, out_buf, in_buf, own_buf, halo_buf,
-                   send_sem, recv_sem, halo_sems):
+def regroup_kernel(n, br, tiles_hbm, ids_hbm, win_ref, tiles_ref, ids_ref, out_buf, in_buf, own_buf, halo_buf,
+                   send_sem, recv_sem, halo_sems, load_sems):
     count = tiles_ref.shape[0]
+    load_ids = pltpu.make_async_copy(ids_hbm, ids_ref, load_sems.at[0])
+    load_tiles = pltpu.make_async_copy(tiles_hbm, tiles_ref, load_sems.at[1])
+    load_ids.start()
+    load_tiles.start()
     me = lax.axis_index("tm")
     barrier = pltpu.get_barrier_semaphore()
 
@@ -31,6 +35,7 @@
 
     lax.fori_loop(1, n, greet, 0)
 
+    load_ids.wait()
     ids = ids_ref[...].astype(F32)
     target = jnp.floor((ids + 0.5) * (1.0 / count))
     slot = ids - target * count
@@ -46,6 +51,7 @@
     lanes_at = jnp.where((iota((count, 128), 1) % br).astype(F32) == rank_col, 1.0, 0.0).astype(BF16)
     slot_rows = jnp.dot(slots_at, lanes_at, preferred_element_type=F32).astype(BF16)
     last = jnp.where(iota((total, n), 0) == iota((total, n), 1) * br + br - 1, 1.0, 0.0).astype(BF16)
+    load_tiles.wait()
     outbound = jnp.dot(spread, tiles_ref[...].astype(BF16), preferred_element_type=F32)
     outbound = outbound + jnp.dot(last, slot_rows, preferred_element_type=F32)
     out_buf[...] = outbound.astype(BF16).reshape(n, br, 128)
@@ -91,21 +97,27 @@
     win_ref[:count] = halo_buf[...]
 
 
-def silu_norm(values, gain):
-    normed = values * lax.rsqrt(jnp.mean(values * values, axis=-1, keepdims=True) + 1e-06)
-    scaled = normed * gain
-    return scaled / (1.0 + jnp.exp(-scaled))
-
-
-def decode_kernel(win_ref, count_ref, w_in_ref, b_in_ref, g_one_ref, w_res_ref, b_res_ref, g_two_ref,
-                  block_ref, branch_ref, w_buf, lat, lhs, edge, toep, pre, acts, acc, masks, sems):
-    c = b_in_ref.shape[1]
+def silu_norm(values, half_gain):
+    half = values * lax.rsqrt(jnp.mean(values * values, axis=-1, keepdims=True) + 1e-06) * half_gain
+    return half + half * jnp.tanh(half)
+
+
+def decode_kernel(win_hbm, count_ref, w_in_hbm, b_in_ref, g_one_ref, w_res_ref, b_res_ref, g_two_ref,
+                  block_hbm, branch_hbm, win_ref, w_in_ref, block_ref, branch_ref, w_buf, lat, lhs, edge, toep, pre,
+                  acts, masks, sems, load_sems, out_sems):
+    c = b_in_ref.shape[0]
+    load_w_in = pltpu.make_async_copy(w_in_hbm, w_in_ref, load_sems.at[0])
+    load_win = pltpu.make_async_copy(win_hbm, win_ref, load_sems.at[1])
+    load_w_in.start()
+    load_win.start()
+    bias_one, bias_two = b_in_ref[...].reshape(1, c), b_res_ref[...].reshape(1, c)
+    gain_one, gain_two = 0.5 * g_one_ref[...].reshape(1, c), 0.5 * g_two_ref[...].reshape(1, c)
     frame = HL * WL
     per_frame = frame // 8
     stride = per_frame + 8
     copies = [
         pltpu.make_async_copy(
-            w_res_ref.at[d, pl.ds(a * 3 * c, 3 * c), :], w_buf.at[d, :, pl.ds(a * c, c)], sems.at[d * 3 + a])
+            w_res_ref.at[d, pl.ds(a * 3 * c, 3 * c), :], w_buf.at[pl.ds(d * 3 * c, 3 * c), pl.ds(a * c, c)], sems.at[d * 3 + a])
         for d in range(3) for a in range(3)
     ]
     for copy in copies:
@@ -123,6 +135,7 @@
         masks[2, g] = jnp.where(first + g - 2 >= begin, 1.0, 0.0)
 
     toep[...] = jnp.zeros_like(toep)
+    load_w_in.wait()
     for d in range(3):
         for a in range(3):
             j = 128 * (3 * d + a)
@@ -135,6 +148,7 @@
             toep[j:j + 16, 9 * c:10 * c] = taps[32:]
 
     lat[...] = jnp.zeros_like(lat)
+    load_win.wait()
     for g in range(LT + 4):
         lat[stride * g + 3:stride * g + 3 + per_frame, :] = win_ref[per_frame * g:per_frame * (g + 1), :].astype(F32)
     row, lane = iota((per_frame, 128), 0) % 3, iota((per_frame, 128), 1)
@@ -166,41 +180,35 @@
 
     column = iota((frame, c), 0) % WL
 
-    def act_frame(g, carry):
-        at = pl.ds(pl.multiple_of(g * frame, frame), frame)
-        rounded = (jnp.concatenate([pre[q, at, :] for q in range(c // 128)], axis=1) + b_in_ref[...]).astype(BF16)
-
-        @pl.when(g >= 2)
-        def _():
+    def act_frame(g):
+        at = slice(g * frame, (g + 1) * frame)
+        rounded = (jnp.concatenate([pre[q, at, :] for q in range(c // 128)], axis=1) + bias_one).astype(BF16)
+        if g >= 2:
             block_ref[g - 2] = rounded
-
-        act = silu_norm(rounded.astype(F32), g_one_ref[...])
+            block_out[g - 2].start()
+        act = silu_norm(rounded.astype(F32), gain_one)
         acts[at, :c] = jnp.where(column == 0, 0.0, pltpu.roll(act, 1, 0)).astype(BF16)
         acts[at, c:2 * c] = act.astype(BF16)
         acts[at, 2 * c:] = jnp.where(column == WL - 1, 0.0, pltpu.roll(act, frame - 1, 0)).astype(BF16)
-        return carry
-
-    lax.fori_loop(0, LT + 2, act_frame, 0)
-
-    acc[...] = jnp.zeros_like(acc)
+
+    block_out = [pltpu.make_async_copy(block_ref.at[f], block_hbm.at[f], out_sems.at[0, f]) for f in range(LT)]
+    branch_out = [pltpu.make_async_copy(branch_ref.at[f], branch_hbm.at[f], out_sems.at[1, f]) for f in range(LT)]
+    for g in range(LT + 2):
+        act_frame(g)
     for copy in copies:
         copy.wait()
 
-    def product(i, carry):
-        d, f = i // LT, i % LT
-        at = pl.ds(pl.multiple_of((f + 2 - d) * frame, frame), frame)
-        out = jnp.dot(acts[at, :], w_buf[d], preferred_element_type=F32) * masks[d, f + 2]
-        for a in range(3):
-            acc[f, WL * (2 - a):WL * (2 - a) + frame, :] += out[:, c * a:c * a + c]
-        return carry
-
-    lax.fori_loop(0, 3 * LT, product, 0)
-
-    def last_frame(f, carry):
-        branch_ref[f] = silu_norm(acc[f, WL:WL + frame, :] + b_res_ref[...], g_two_ref[...]).astype(BF16)
-        return carry
-
-    lax.fori_loop(0, LT, last_frame, 0)
+    blank = jnp.zeros((WL, c), F32)
+    for f in range(LT):
+        taps = [acts[(f + 2 - d) * frame:(f + 3 - d) * frame, :] for d in range(3)]
+        taps = [taps[0]] + [taps[d] * masks[d, f + 2].astype(BF16) for d in (1, 2)]
+        out = jnp.dot(jnp.concatenate(taps, axis=1), w_buf[...], preferred_element_type=F32)
+        above = jnp.concatenate([blank, out[:-WL, :c]], axis=0)
+        below = jnp.concatenate([out[WL:, 2 * c:], blank], axis=0)
+        branch_ref[f] = silu_norm(above + out[:, c:2 * c] + below + bias_two, gain_two).astype(BF16)
+        branch_out[f].start()
+    for copy in block_out + branch_out:
+        copy.wait()
 
 
 def local(
@@ -220,12 +228,15 @@
     cap = max(2, 2 * count // n)
     br = 16 * ((cap + 16) // 16)
     vmem = pl.BlockSpec(memory_space=pltpu.VMEM)
+    anywhere = pl.BlockSpec(memory_space=pl.ANY)
     window = pl.pallas_call(
         functools.partial(regroup_kernel, n, br),
         out_shape=jax.ShapeDtypeStruct((2 * count, 128), BF16),
-        in_specs=[vmem, vmem],
+        in_specs=[anywhere, anywhere],
         out_specs=vmem,
         scratch_shapes=[
+            pltpu.VMEM((count, 128), F32),
+            pltpu.VMEM((1, count), jnp.int32),
             pltpu.VMEM((n, br, 128), BF16),
             pltpu.VMEM((n, br, 128), BF16),
             pltpu.VMEM((count, 128), BF16),
@@ -233,9 +244,10 @@
             pltpu.SemaphoreType.DMA((n,)),
             pltpu.SemaphoreType.DMA((n,)),
             pltpu.SemaphoreType.DMA((2,)),
+            pltpu.SemaphoreType.DMA((2,)),
         ],
         compiler_params=pltpu.CompilerParams(
-            collective_id=0, has_side_effects=True, vmem_limit_bytes=32 * 1024 * 1024),
+            collective_id=0, has_side_effects=True, vmem_limit_bytes=58 * 1024 * 1024),
     )(transformer_tiles, global_tile_index)
 
     frame = HL * WL
@@ -243,25 +255,29 @@
     block_input, branch_act = pl.pallas_call(
         decode_kernel,
         out_shape=[jax.ShapeDtypeStruct((LT, frame, c), BF16)] * 2,
-        in_specs=[vmem, pl.BlockSpec(memory_space=pltpu.SMEM), vmem, vmem, vmem,
-                  pl.BlockSpec(memory_space=pl.ANY), vmem, vmem],
-        out_specs=[vmem, vmem],
+        in_specs=[anywhere, pl.BlockSpec(memory_space=pltpu.SMEM), anywhere, vmem, vmem, anywhere, vmem, vmem],
+        out_specs=[anywhere, anywhere],
         scratch_shapes=[
-            pltpu.VMEM((3, 3 * c, 3 * c), BF16),
+            pltpu.VMEM((2 * count, 128), BF16),
+            pltpu.VMEM(input_conv_weight.shape, F32),
+            pltpu.VMEM((LT, frame, c), BF16),
+            pltpu.VMEM((LT, frame, c), BF16),
+            pltpu.VMEM((9 * c, 3 * c), BF16),
             pltpu.VMEM(((LT + 4) * (frame // 8 + 8), 128), F32),
             pltpu.VMEM((act_rows // 8, 9 * 128), BF16),
             pltpu.VMEM((act_rows // 8, 9 * 128), BF16),
             pltpu.VMEM((9 * 128, 10 * c), BF16),
             pltpu.VMEM((c // 128, act_rows, 128), F32),
             pltpu.VMEM((act_rows, 3 * c), BF16),
-            pltpu.VMEM((LT, frame + 2 * WL, c), F32),
             pltpu.SMEM((3, LT + 2), F32),
             pltpu.SemaphoreType.DMA((9,)),
+            pltpu.SemaphoreType.DMA((2,)),
+            pltpu.SemaphoreType.DMA((2, LT)),
         ],
         compiler_params=pltpu.CompilerParams(vmem_limit_bytes=58 * 1024 * 1024),
         cost_estimate=pl.CostEstimate(flops=16_000_000_000, bytes_accessed=12_000_000, transcendentals=2_000_000),
-    )(window, video_frame_count, input_conv_weight, input_conv_bias[None], first_norm_gain[None],
-      residual_conv_weight, residual_conv_bias[None], second_norm_gain[None])
+    )(window, video_frame_count, input_conv_weight, input_conv_bias, first_norm_gain,
+      residual_conv_weight, residual_conv_bias, second_norm_gain)
     return (block_input.reshape(LT, HL, WL, c), branch_act.reshape(LT, HL, WL, c))
 
 

time: 51.9 us -> 43.3 us (0.83)
  local copies, waits for them, and re-layouts: 7.19 us -> 0 us
  Pallas kernels: 43.8 us -> 42.4 us
    broadcast_in_dim x4 -> x0, local copies, waits for them, and re-layouts: 5 us -> none  [the longest x1 1.26 us: local(): first_norm_gain[None]]
    unnamed x6 -> x0, local copies, waits for them, and re-layouts: 2.19 us -> none
    pallas_call x1, Pallas kernels: 27.9 us -> 25.8 us  [local(): pl.pallas_call(decode_kernel, out_shape=[jax.ShapeDtypeStruct((LT, frame,...]
    pallas_call x1, Pallas kernels: 15.9 us -> 16.6 us  [local(): pl.pallas_call(functools.partial(regroup_kernel, n, br), out_shape=jax.Sh...]
where the time goes in v1:
time: 43.3 us; the launch traced here: 43.2 us
  Pallas kernels  42.4 us (98%)
  between operations  0.8 us (2%)
    pallas_call x1, Pallas kernels, local(): pl.pallas_call(decode_kernel, out_shape=[jax.ShapeDtypeStruct((LT, frame,...  25.8 us
    pallas_call x1, Pallas kernels, local(): pl.pallas_call(functools.partial(regroup_kernel, n, br), out_shape=jax.Sh...  16.6 us

profile of v1, /device:TPU:0, one launch (start us, length us, event | category | flops | bytes accessed | tf_op | source)
XLA Modules:
  0.0 43.2 jit_solution(2560213537241076222)
XLA Ops:
  0.6 16.6 %shard_map.104.win_hbm = bf16[384,128]{1,0:T(8,128)(2,1)} custom-call(f32[192,128]{1,0:T(8,128)} %tiles_hbm.1, s32[1,192]{1,0:T(1,128)} %ids_hbm.1), custom_call_target="tpu_custom_call" | custom-call | tf_op jit(solution)/shard_map/pallas_call | solution.py:232
  17.3 25.8 %shard_map.105 = (bf16[4,384,384]{2,1,0:T(8,128)(2,1)}, bf16[4,384,384]{2,1,0:T(8,128)(2,1)}) custom-call(bf16[384,128]{1,0:T(8,128)(2,1)} %shard_map.104.win_hbm, s32[8]{0:T(128)} %count_ref.1, f32[3,144,384]{2,1,0:T(8,128)} %w_in_hbm.1, f32[384]{0:T(512)} %b_in_ref.1, f32[384]{0:T(512)} %g_one_ref.1, bf16[3,3456,384]{2,1,0:T(8,128)(2,1)} %w_res_ref.1, ...), custom_call_target="tpu_custom_call" | custom-call | flops 16000000000 | bytes 12000000 | tf_op jit(solution)/shard_map/pallas_call | solution.py:255

commit v2 on v1

v2 whole, which is shorter than its diff:
```python
import functools

import jax
import jax.numpy as jnp
from jax import lax
from jax.experimental import pallas as pl
from jax.experimental.pallas import tpu as pltpu
from jax.sharding import PartitionSpec as P

LT = 4
HL = 16
WL = 24
MESH = pl.DeviceIdType.MESH
F32 = jnp.float32
BF16 = jnp.bfloat16


def iota(shape, dim):
    return lax.broadcasted_iota(jnp.int32, shape, dim)


def regroup_kernel(n, br, tiles_hbm, ids_hbm, count_ref, w_in_hbm, b_in_ref, out_ref, tiles_ref, ids_ref, w_in_ref,
                   out_buf, in_buf, own_buf, halo_buf, lat, lhs, edge, toep, pre, masks,
                   send_sem, recv_sem, halo_sems, load_sems):
    count = tiles_ref.shape[0]
    load_ids = pltpu.make_async_copy(ids_hbm, ids_ref, load_sems.at[0])
    load_tiles = pltpu.make_async_copy(tiles_hbm, tiles_ref, load_sems.at[1])
    load_w_in = pltpu.make_async_copy(w_in_hbm, w_in_ref, load_sems.at[2])
    load_ids.start()
    load_tiles.start()
    load_w_in.start()
    me = lax.axis_index("tm")
    barrier = pltpu.get_barrier_semaphore()

    def greet(k, carry):
        pl.semaphore_signal(barrier, inc=1, device_id={"tm": lax.rem(me + k, n)}, device_id_type=MESH)
        return carry

    lax.fori_loop(1, n, greet, 0)

    load_ids.wait()
    ids = ids_ref[...].astype(F32)
    target = jnp.floor((ids + 0.5) * (1.0 / count))
    slot = ids - target * count
    rows, cols = iota((count, count), 0), iota((count, count), 1)
    target_col = jnp.sum(jnp.where(rows == cols, target, 0.0), axis=1, keepdims=True)
    same = (target_col == target) & (rows < cols)
    rank = jnp.sum(jnp.where(same, 1.0, 0.0), axis=0, keepdims=True)
    rank_col = jnp.sum(jnp.where(rows == cols, rank, 0.0), axis=1, keepdims=True)
    position = target * br + rank
    total = n * br
    spread = jnp.where(iota((total, count), 0).astype(F32) == position, 1.0, 0.0).astype(BF16)
    slots_at = jnp.where(iota((n, count), 0).astype(F32) == target, slot + 1.0, 0.0).astype(BF16)
    lanes_at = jnp.where((iota((count, 128), 1) % br).astype(F32) == rank_col, 1.0, 0.0).astype(BF16)
    slot_rows = jnp.dot(slots_at, lanes_at, preferred_element_type=F32).astype(BF16)
    last = jnp.where(iota((total, n), 0) == iota((total, n), 1) * br + br - 1, 1.0, 0.0).astype(BF16)
    load_tiles.wait()
    outbound = jnp.dot(spread, tiles_ref[...].astype(BF16), preferred_element_type=F32)
    outbound = outbound + jnp.dot(last, slot_rows, preferred_element_type=F32)
    out_buf[...] = outbound.astype(BF16).reshape(n, br, 128)

    pl.semaphore_wait(barrier, n - 1)

    def block_copy(k):
        peer = lax.rem(me + k, n)
        return pltpu.make_async_remote_copy(
            src_ref=out_buf.at[peer], dst_ref=in_buf.at[me], send_sem=send_sem.at[k],
            recv_sem=recv_sem.at[k], device_id={"tm": peer}, device_id_type=MESH)

    def start(k, carry):
        block_copy(k).start()
        return carry

    def finish(k, carry):
        block_copy(k).wait()
        return carry

    lax.fori_loop(1, n, start, 0)
    in_buf[me] = out_buf[me]

    c = b_in_ref.shape[0]
    frame = HL * WL
    per_frame = frame // 8
    stride = per_frame + 8
    first = me * LT - 2
    for g in range(LT + 2):
        begin = jnp.int32(0)
        bound = jnp.int32(0)
        for v in range(count_ref.shape[0]):
            begin = jnp.where(bound <= first + g, bound, begin)
            bound = bound + count_ref[v]
        masks[0, g] = 1.0
        masks[1, g] = jnp.where(first + g - 1 >= begin, 1.0, 0.0)
        masks[2, g] = jnp.where(first + g - 2 >= begin, 1.0, 0.0)
    toep[...] = jnp.zeros_like(toep)
    lat[...] = jnp.zeros_like(lat)
    load_w_in.wait()
    for d in range(3):
        for a in range(3):
            j = 128 * (3 * d + a)
            taps = w_in_ref[d, 48 * a:48 * a + 48, :].astype(BF16)
            for x in range(8):
                low, high = max(0, x - 1), min(7, x + 1)
                skip = 16 * (low - x + 1)
                toep[j + 16 * low:j + 16 * high + 16, c * x:c * x + c] = taps[skip:skip + 16 * (high - low + 1)]
            toep[j + 112:j + 128, 8 * c:9 * c] = taps[:16]
            toep[j:j + 16, 9 * c:10 * c] = taps[32:]

    lax.fori_loop(1, n, finish, 0)

    incoming = in_buf[...].reshape(total, 128)
    pick = jnp.where(iota((n, total), 1) == iota((n, total), 0) * br + br - 1, 1.0, 0.0).astype(BF16)
    in_slots = jnp.dot(pick, incoming, preferred_element_type=F32)
    per_tile = 128 // br
    pieces = []
    for k in range(total // 128):
        own = iota((n, 128), 0) == k * per_tile + iota((n, 128), 1) // br
        slot_row = jnp.sum(jnp.where(own, in_slots, 0.0), axis=0, keepdims=True)
        hit = iota((count, 128), 0).astype(F32) + 1.0 == slot_row
        pieces.append(jnp.where(hit, 1.0, 0.0).astype(BF16))
    gather = jnp.concatenate(pieces, axis=1)
    own_buf[...] = jnp.dot(gather, incoming, preferred_element_type=F32).astype(BF16)
    halo = pltpu.make_async_remote_copy(
        src_ref=own_buf, dst_ref=halo_buf, send_sem=halo_sems.at[0], recv_sem=halo_sems.at[1],
        device_id={"tm": lax.rem(me + 1, n)}, device_id_type=MESH)
    halo.start()

    row, lane = iota((per_frame, 128), 0) % 3, iota((per_frame, 128), 1)
    from_right = (lane < 16) & (row != 2)
    from_left = (lane >= 112) & (row != 0)

    def fill(source, begin):
        for g in range(LT):
            at = stride * (g + begin) + 3
            lat[at:at + per_frame, :] = source[per_frame * g:per_frame * (g + 1), :].astype(F32)

    def operand(own):
        for g in range(LT + 2):
            for d in range(3):
                if (g + 2 - d >= LT) != own:
                    continue
                for a in range(3):
                    j = 128 * (3 * d + a)
                    base = stride * (g + 2 - d) + 3 * a
                    piece = lat[base:base + per_frame, :] * masks[d, g]
                    lhs[per_frame * g:per_frame * (g + 1), j:j + 128] = piece.astype(BF16)
                    beside = jnp.where(from_right, pltpu.roll(piece, per_frame - 1, 0),
                                       jnp.where(from_left, pltpu.roll(piece, 1, 0), 0.0))
                    edge[per_frame * g:per_frame * (g + 1), j:j + 128] = beside.astype(BF16)

    fill(own_buf, LT)
    operand(True)
    halo.wait()
    fill(halo_buf, 0)
    operand(False)

    rows = per_frame * (LT + 2)
    sides = jnp.dot(edge[...], toep[:, 8 * c:], preferred_element_type=F32)
    for p in range(4):
        out = jnp.dot(lhs[...], toep[:, 2 * c * p:2 * c * (p + 1)], preferred_element_type=F32)
        even, odd = out[:, :c], out[:, c:]
        if p == 0:
            even = even + sides[:, :c]
        if p == 3:
            odd = odd + sides[:, c:]
        for e, part in enumerate((even, odd)):
            for q in range(c // 128):
                pre[q, pl.ds(2 * p + e, rows, stride=8), :] = part[:, 128 * q:128 * q + 128]
    for q in range(c // 128):
        bias = b_in_ref[128 * q:128 * q + 128].reshape(1, 128)
        out_ref[:, 128 * q:128 * q + 128] = (pre[q] + bias).astype(BF16)


def silu_norm(values, half_gain):
    half = values * lax.rsqrt(jnp.mean(values * values, axis=-1, keepdims=True) + 1e-06) * half_gain
    return half + half * jnp.tanh(half)


def decode_kernel(input_hbm, count_ref, g_one_ref, w_res_ref, b_res_ref, g_two_ref, block_hbm, branch_hbm,
                  w_buf, in_frames, out_frames, act_refs, sums, masks, w_sems, in_sems, out_sems, block_sem):
    c = b_res_ref.shape[0]
    frame = HL * WL
    part = frame // 4
    load_in = [
        pltpu.make_async_copy(input_hbm.at[pl.ds(g * frame, frame), :], in_frames[g], in_sems.at[g])
        for g in range(LT + 2)
    ]
    load_w = [
        pltpu.make_async_copy(
            w_res_ref.at[d, pl.ds(a * 3 * c, 3 * c), :],
            w_buf.at[pl.ds(d * 3 * c, 3 * c), pl.ds(a * c, c)], w_sems.at[d * 3 + a])
        for d in range(3) for a in range(3)
    ]
    block_out = pltpu.make_async_copy(input_hbm.at[pl.ds(2 * frame, LT * frame), :], block_hbm, block_sem)
    branch_out = [
        pltpu.make_async_copy(out_frames[f], branch_hbm.at[pl.ds(f * frame, frame), :], out_sems.at[f])
        for f in range(LT)
    ]
    for copy in load_in + load_w + [block_out]:
        copy.start()
    bias_two = b_res_ref[...].reshape(1, c)
    gain_one, gain_two = 0.5 * g_one_ref[...].reshape(1, c), 0.5 * g_two_ref[...].reshape(1, c)
    column = iota((part, c), 0) % WL

    first = lax.axis_index("tm") * LT
    for f in range(LT):
        begin = jnp.int32(0)
        bound = jnp.int32(0)
        for v in range(count_ref.shape[0]):
            begin = jnp.where(bound <= first + f, bound, begin)
            bound = bound + count_ref[v]
        masks[0, f] = jnp.where(first + f - 1 >= begin, 1.0, 0.0)
        masks[1, f] = jnp.where(first + f - 2 >= begin, 1.0, 0.0)

    def act_part(g, i):
        if i == 0:
            load_in[g].wait()
        at = slice(i * part, (i + 1) * part)
        act = silu_norm(in_frames[g][at, :].astype(F32), gain_one)
        act_refs[g][at, :c] = jnp.where(column == 0, 0.0, pltpu.roll(act, 1, 0)).astype(BF16)
        act_refs[g][at, c:2 * c] = act.astype(BF16)
        act_refs[g][at, 2 * c:] = jnp.where(column == WL - 1, 0.0, pltpu.roll(act, part - 1, 0)).astype(BF16)

    def finish_part(f, i):
        low, high = i * part, (i + 1) * part
        out = sums[f % 2]
        blank = jnp.zeros((WL, c), F32)
        above = out[low - WL:high - WL, :c] if i > 0 else jnp.concatenate([blank, out[:high - WL, :c]], axis=0)
        below = out[low + WL:high + WL, 2 * c:] if i < 3 else jnp.concatenate([out[low + WL:, 2 * c:], blank], axis=0)
        total = above + out[low:high, c:2 * c] + below + bias_two
        out_frames[f][low:high, :] = silu_norm(total, gain_two).astype(BF16)
        if i == 3:
            branch_out[f].start()

    def product_part(f, low, high):
        taps = [act_refs[f + 2][...]]
        taps += [act_refs[f + 2 - d][...] * masks[d - 1, f].astype(BF16) for d in (1, 2)]
        sums[f % 2][:, low:high] = jnp.dot(
            jnp.concatenate(taps, axis=1), w_buf[:, low:high], preferred_element_type=F32)

    for g in range(3):
        for i in range(4):
            act_part(g, i)
    for copy in load_w:
        copy.wait()
    cuts = list(range(0, 3 * c, 256)) + [3 * c]
    for f in range(LT):
        beside = [functools.partial(finish_part, f - 1, i) for i in range(4)] if f > 0 else []
        beside += [functools.partial(act_part, f + 3, i) for i in range(4)] if f < LT - 1 else []
        steps = len(cuts) - 1
        for k in range(steps):
            product_part(f, cuts[k], cuts[k + 1])
            for work in beside[len(beside) * k // steps:len(beside) * (k + 1) // steps]:
                work()
    for i in range(4):
        finish_part(LT - 1, i)
    for copy in branch_out + [block_out]:
        copy.wait()


def local(
    transformer_tiles,
    global_tile_index,
    video_frame_count,
    input_conv_weight,
    input_conv_bias,
    first_norm_gain,
    residual_conv_weight,
    residual_conv_bias,
    second_norm_gain,
):
    n = lax.axis_size("tm")
    count = transformer_tiles.shape[0]
    c = input_conv_bias.shape[0]
    cap = max(2, 2 * count // n)
    br = 16 * ((cap + 16) // 16)
    vmem = pl.BlockSpec(memory_space=pltpu.VMEM)
    anywhere = pl.BlockSpec(memory_space=pl.ANY)
    frame = HL * WL
    act_rows = (LT + 2) * frame
    smem = pl.BlockSpec(memory_space=pltpu.SMEM)
    rounded = pl.pallas_call(
        functools.partial(regroup_kernel, n, br),
        out_shape=jax.ShapeDtypeStruct((act_rows, c), BF16),
        in_specs=[anywhere, anywhere, smem, anywhere, vmem],
        out_specs=vmem,
        scratch_shapes=[
            pltpu.VMEM((count, 128), F32),
            pltpu.VMEM((1, count), jnp.int32),
            pltpu.VMEM(input_conv_weight.shape, F32),
            pltpu.VMEM((n, br, 128), BF16),
            pltpu.VMEM((n, br, 128), BF16),
            pltpu.VMEM((count, 128), BF16),
            pltpu.VMEM((count, 128), BF16),
            pltpu.VMEM(((LT + 4) * (frame // 8 + 8), 128), F32),
            pltpu.VMEM((act_rows // 8, 9 * 128), BF16),
            pltpu.VMEM((act_rows // 8, 9 * 128), BF16),
            pltpu.VMEM((9 * 128, 10 * c), BF16),
            pltpu.VMEM((c // 128, act_rows, 128), F32),
            pltpu.SMEM((3, LT + 2), F32),
            pltpu.SemaphoreType.DMA((n,)),
            pltpu.SemaphoreType.DMA((n,)),
            pltpu.SemaphoreType.DMA((2,)),
            pltpu.SemaphoreType.DMA((3,)),
        ],
        compiler_params=pltpu.CompilerParams(
            collective_id=0, has_side_effects=True, vmem_limit_bytes=58 * 1024 * 1024),
    )(transformer_tiles, global_tile_index, video_frame_count, input_conv_weight, input_conv_bias)

    block_input, branch_act = pl.pallas_call(
        decode_kernel,
        out_shape=[jax.ShapeDtypeStruct((LT * frame, c), BF16)] * 2,
        in_specs=[anywhere, smem, vmem, anywhere, vmem, vmem],
        out_specs=[anywhere, anywhere],
        scratch_shapes=[
            pltpu.VMEM((9 * c, 3 * c), BF16),
            [pltpu.VMEM((frame, c), BF16) for _ in range(LT + 2)],
            [pltpu.VMEM((frame, c), BF16) for _ in range(LT)],
            [pltpu.VMEM((frame, 3 * c), BF16) for _ in range(LT + 2)],
            [pltpu.VMEM((frame, 3 * c), F32) for _ in range(2)],
            pltpu.SMEM((2, LT), F32),
            pltpu.SemaphoreType.DMA((9,)),
            pltpu.SemaphoreType.DMA((LT + 2,)),
            pltpu.SemaphoreType.DMA((LT,)),
            pltpu.SemaphoreType.DMA,
        ],
        compiler_params=pltpu.CompilerParams(vmem_limit_bytes=58 * 1024 * 1024),
        cost_estimate=pl.CostEstimate(flops=16_000_000_000, bytes_accessed=12_000_000, transcendentals=2_000_000),
    )(rounded, video_frame_count, first_norm_gain, residual_conv_weight, residual_conv_bias, second_norm_gain)
    return (block_input.reshape(LT, HL, WL, c), branch_act.reshape(LT, HL, WL, c))


def solution(mesh):
    placed = (
        P(("grp", "tm"), None),
        P(("grp", "tm"), None),
        P("grp"),
        P(),
        P(),
        P(),
        P(),
        P(),
        P(),
    )
    return jax.shard_map(
        local,
        mesh=mesh,
        in_specs=placed,
        out_specs=(P(("grp", "tm"), None, None, None), P(("grp", "tm"), None, None, None)),
        check_vma=False,
    )
```

time: 43.3 us -> 60.2 us (1.39)
  Pallas kernels: 42.4 us -> 59.2 us
    pallas_call x1, Pallas kernels: 25.8 us -> 37.8 us  [local(): pl.pallas_call(decode_kernel, out_shape=[jax.ShapeDtypeStruct((LT * frame...]
    pallas_call x1, Pallas kernels: 16.6 us -> 21.4 us  [local(): pl.pallas_call(functools.partial(regroup_kernel, n, br), out_shape=jax.Sh...]
where the time goes in v2:
time: 60.2 us; the launch traced here: 60 us
  Pallas kernels  59.2 us (98%)
  between operations  0.8 us (1%)
    pallas_call x1, Pallas kernels, local(): pl.pallas_call(decode_kernel, out_shape=[jax.ShapeDtypeStruct((LT * frame...  37.8 us
    pallas_call x1, Pallas kernels, local(): pl.pallas_call(functools.partial(regroup_kernel, n, br), out_shape=jax.Sh...  21.4 us

profile of v2, /device:TPU:0, one launch (start us, length us, event | category | flops | bytes accessed | tf_op | source)
XLA Modules:
  0.0 60.0 jit_solution(11423624370298972110)
XLA Ops:
  0.6 21.4 %shard_map.104.input_hbm = bf16[2304,384]{1,0:T(8,128)(2,1)} custom-call(f32[192,128]{1,0:T(8,128)} %tiles_hbm.1, s32[1,192]{1,0:T(1,128)} %ids_hbm.1, s32[8]{0:T(128)} %count_ref.3, f32[3,144,384]{2,1,0:T(8,128)} %w_in_hbm.1, f32[384]{0:T(512)} %b_in_ref.1), custom_call_target="tpu_custom_call" | custom-call | tf_op jit(solution)/shard_map/pallas_call | solution.py:282
  22.0 37.8 %shard_map.105 = (bf16[1536,384]{1,0:T(8,128)(2,1)}, bf16[1536,384]{1,0:T(8,128)(2,1)}) custom-call(bf16[2304,384]{1,0:T(8,128)(2,1)} %shard_map.104.input_hbm, s32[8]{0:T(128)} %count_ref.3, f32[384]{0:T(512)} %g_one_ref.1, bf16[3,3456,384]{2,1,0:T(8,128)(2,1)} %w_res_ref.1, f32[384]{0:T(512)} %b_res_ref.1, f32[384]{0:T(512)} %g_two_ref.1), custom_call_target="tpu_custom_call" | custom-call | flops 16000000000 | bytes 12000000 | tf_op jit(solution)/shard_map/pallas_call | solution.py:310

commit v3 on v2

--- a/solution.py
+++ b/solution.py
@@ -177,7 +177,7 @@
 
 
 def decode_kernel(input_hbm, count_ref, g_one_ref, w_res_ref, b_res_ref, g_two_ref, block_hbm, branch_hbm,
-                  w_buf, in_frames, out_frames, act_refs, sums, masks, w_sems, in_sems, out_sems, block_sem):
+                  w_buf, in_frames, out_frames, operands, sums, masks, w_sems, in_sems, out_sems, block_sem):
     c = b_res_ref.shape[0]
     frame = HL * WL
     part = frame // 4
@@ -217,9 +217,13 @@
             load_in[g].wait()
         at = slice(i * part, (i + 1) * part)
         act = silu_norm(in_frames[g][at, :].astype(F32), gain_one)
-        act_refs[g][at, :c] = jnp.where(column == 0, 0.0, pltpu.roll(act, 1, 0)).astype(BF16)
-        act_refs[g][at, c:2 * c] = act.astype(BF16)
-        act_refs[g][at, 2 * c:] = jnp.where(column == WL - 1, 0.0, pltpu.roll(act, part - 1, 0)).astype(BF16)
+        left = jnp.where(column == 0, 0.0, pltpu.roll(act, 1, 0)).astype(BF16)
+        right = jnp.where(column == WL - 1, 0.0, pltpu.roll(act, part - 1, 0)).astype(BF16)
+        for k, values in enumerate((left, act.astype(BF16), right)):
+            for d in range(3):
+                if 0 <= g - 2 + d < LT:
+                    scaled = values if d == 0 else values * masks[d - 1, g - 2 + d].astype(BF16)
+                    operands[g - 2 + d][at, (3 * d + k) * c:(3 * d + k + 1) * c] = scaled
 
     def finish_part(f, i):
         low, high = i * part, (i + 1) * part
@@ -232,26 +236,18 @@
         if i == 3:
             branch_out[f].start()
 
-    def product_part(f, low, high):
-        taps = [act_refs[f + 2][...]]
-        taps += [act_refs[f + 2 - d][...] * masks[d - 1, f].astype(BF16) for d in (1, 2)]
-        sums[f % 2][:, low:high] = jnp.dot(
-            jnp.concatenate(taps, axis=1), w_buf[:, low:high], preferred_element_type=F32)
-
     for g in range(3):
         for i in range(4):
             act_part(g, i)
     for copy in load_w:
         copy.wait()
-    cuts = list(range(0, 3 * c, 256)) + [3 * c]
     for f in range(LT):
-        beside = [functools.partial(finish_part, f - 1, i) for i in range(4)] if f > 0 else []
-        beside += [functools.partial(act_part, f + 3, i) for i in range(4)] if f < LT - 1 else []
-        steps = len(cuts) - 1
-        for k in range(steps):
-            product_part(f, cuts[k], cuts[k + 1])
-            for work in beside[len(beside) * k // steps:len(beside) * (k + 1) // steps]:
-                work()
+        sums[f % 2][...] = jnp.dot(operands[f][...], w_buf[...], preferred_element_type=F32)
+        for i in range(4):
+            if f < LT - 1:
+                act_part(f + 3, i)
+            if f > 0:
+                finish_part(f - 1, i)
     for i in range(4):
         finish_part(LT - 1, i)
     for copy in branch_out + [block_out]:
@@ -316,7 +312,7 @@
             pltpu.VMEM((9 * c, 3 * c), BF16),
             [pltpu.VMEM((frame, c), BF16) for _ in range(LT + 2)],
             [pltpu.VMEM((frame, c), BF16) for _ in range(LT)],
-            [pltpu.VMEM((frame, 3 * c), BF16) for _ in range(LT + 2)],
+            [pltpu.VMEM((frame, 9 * c), BF16) for _ in range(LT)],
             [pltpu.VMEM((frame, 3 * c), F32) for _ in range(2)],
             pltpu.SMEM((2, LT), F32),
             pltpu.SemaphoreType.DMA((9,)),

time: 60.2 us -> 60.2 us (level)
  no operation moved by 1% of the time
where the time goes in v3:
time: 60.2 us; the launch traced here: 60 us
  Pallas kernels  59.2 us (98%)
  between operations  0.8 us (1%)
    pallas_call x1, Pallas kernels, local(): pl.pallas_call(decode_kernel, out_shape=[jax.ShapeDtypeStruct((LT * frame...  37.8 us
    pallas_call x1, Pallas kernels, local(): pl.pallas_call(functools.partial(regroup_kernel, n, br), out_shape=jax.Sh...  21.4 us

profile of v3, /device:TPU:0, one launch (start us, length us, event | category | flops | bytes accessed | tf_op | source)
XLA Modules:
  0.0 60.0 jit_solution(14490910470600332219)
XLA Ops:
  0.6 21.4 %shard_map.104.input_hbm = bf16[2304,384]{1,0:T(8,128)(2,1)} custom-call(f32[192,128]{1,0:T(8,128)} %tiles_hbm.1, s32[1,192]{1,0:T(1,128)} %ids_hbm.1, s32[8]{0:T(128)} %count_ref.3, f32[3,144,384]{2,1,0:T(8,128)} %w_in_hbm.1, f32[384]{0:T(512)} %b_in_ref.1), custom_call_target="tpu_custom_call" | custom-call | tf_op jit(solution)/shard_map/pallas_call | solution.py:278
  22.0 37.8 %shard_map.105 = (bf16[1536,384]{1,0:T(8,128)(2,1)}, bf16[1536,384]{1,0:T(8,128)(2,1)}) custom-call(bf16[2304,384]{1,0:T(8,128)(2,1)} %shard_map.104.input_hbm, s32[8]{0:T(128)} %count_ref.3, f32[384]{0:T(512)} %g_one_ref.1, bf16[3,3456,384]{2,1,0:T(8,128)(2,1)} %w_res_ref.1, f32[384]{0:T(512)} %b_res_ref.1, f32[384]{0:T(512)} %g_two_ref.1), custom_call_target="tpu_custom_call" | custom-call | flops 16000000000 | bytes 12000000 | tf_op jit(solution)/shard_map/pallas_call | solution.py:306

commit v4 on v3

--- a/solution.py
+++ b/solution.py
@@ -177,7 +177,7 @@
 
 
 def decode_kernel(input_hbm, count_ref, g_one_ref, w_res_ref, b_res_ref, g_two_ref, block_hbm, branch_hbm,
-                  w_buf, in_frames, out_frames, operands, sums, masks, w_sems, in_sems, out_sems, block_sem):
+                  w_buf, in_frames, out_frames, operands, sums, masks, w_sems, in_sems, out_sems, block_sems):
     c = b_res_ref.shape[0]
     frame = HL * WL
     part = frame // 4
@@ -191,12 +191,15 @@
             w_buf.at[pl.ds(d * 3 * c, 3 * c), pl.ds(a * c, c)], w_sems.at[d * 3 + a])
         for d in range(3) for a in range(3)
     ]
-    block_out = pltpu.make_async_copy(input_hbm.at[pl.ds(2 * frame, LT * frame), :], block_hbm, block_sem)
+    block_out = [
+        pltpu.make_async_copy(in_frames[f + 2], block_hbm.at[pl.ds(f * frame, frame), :], block_sems.at[f])
+        for f in range(LT)
+    ]
     branch_out = [
         pltpu.make_async_copy(out_frames[f], branch_hbm.at[pl.ds(f * frame, frame), :], out_sems.at[f])
         for f in range(LT)
     ]
-    for copy in load_in + load_w + [block_out]:
+    for copy in load_in + load_w:
         copy.start()
     bias_two = b_res_ref[...].reshape(1, c)
     gain_one, gain_two = 0.5 * g_one_ref[...].reshape(1, c), 0.5 * g_two_ref[...].reshape(1, c)
@@ -215,6 +218,8 @@
     def act_part(g, i):
         if i == 0:
             load_in[g].wait()
+            if g >= 2:
+                block_out[g - 2].start()
         at = slice(i * part, (i + 1) * part)
         act = silu_norm(in_frames[g][at, :].astype(F32), gain_one)
         left = jnp.where(column == 0, 0.0, pltpu.roll(act, 1, 0)).astype(BF16)
@@ -250,7 +255,7 @@
                 finish_part(f - 1, i)
     for i in range(4):
         finish_part(LT - 1, i)
-    for copy in branch_out + [block_out]:
+    for copy in branch_out + block_out:
         copy.wait()
 
 
@@ -318,7 +323,7 @@
             pltpu.SemaphoreType.DMA((9,)),
             pltpu.SemaphoreType.DMA((LT + 2,)),
             pltpu.SemaphoreType.DMA((LT,)),
-            pltpu.SemaphoreType.DMA,
+            pltpu.SemaphoreType.DMA((LT,)),
         ],
         compiler_params=pltpu.CompilerParams(vmem_limit_bytes=58 * 1024 * 1024),
         cost_estimate=pl.CostEstimate(flops=16_000_000_000, bytes_accessed=12_000_000, transcendentals=2_000_000),

time: 60.2 us -> 47.2 us (0.78)
  Pallas kernels: 59.2 us -> 46.2 us
    pallas_call x1, Pallas kernels: 37.8 us -> 24.8 us  [local(): pl.pallas_call(decode_kernel, out_shape=[jax.ShapeDtypeStruct((LT * frame...]
where the time goes in v4:
time: 47.2 us; the launch traced here: 47 us
  Pallas kernels  46.2 us (98%)
  between operations  0.8 us (2%)
    pallas_call x1, Pallas kernels, local(): pl.pallas_call(decode_kernel, out_shape=[jax.ShapeDtypeStruct((LT * frame...  24.8 us
    pallas_call x1, Pallas kernels, local(): pl.pallas_call(functools.partial(regroup_kernel, n, br), out_shape=jax.Sh...  21.4 us

profile of v4, /device:TPU:0, one launch (start us, length us, event | category | flops | bytes accessed | tf_op | source)
XLA Modules:
  0.0 47.0 jit_solution(8281467660187051279)
XLA Ops:
  0.6 21.4 %shard_map.104.input_hbm = bf16[2304,384]{1,0:T(8,128)(2,1)} custom-call(f32[192,128]{1,0:T(8,128)} %tiles_hbm.1, s32[1,192]{1,0:T(1,128)} %ids_hbm.1, s32[8]{0:T(128)} %count_ref.3, f32[3,144,384]{2,1,0:T(8,128)} %w_in_hbm.1, f32[384]{0:T(512)} %b_in_ref.1), custom_call_target="tpu_custom_call" | custom-call | tf_op jit(solution)/shard_map/pallas_call | solution.py:283
  22.0 24.8 %shard_map.105 = (bf16[1536,384]{1,0:T(8,128)(2,1)}, bf16[1536,384]{1,0:T(8,128)(2,1)}) custom-call(bf16[2304,384]{1,0:T(8,128)(2,1)} %shard_map.104.input_hbm, s32[8]{0:T(128)} %count_ref.3, f32[384]{0:T(512)} %g_one_ref.1, bf16[3,3456,384]{2,1,0:T(8,128)(2,1)} %w_res_ref.1, f32[384]{0:T(512)} %b_res_ref.1, f32[384]{0:T(512)} %g_two_ref.1), custom_call_target="tpu_custom_call" | custom-call | flops 16000000000 | bytes 12000000 | tf_op jit(solution)/shard_map/pallas_call | solution.py:311

commit v5 on v1

--- a/solution.py
+++ b/solution.py
@@ -103,8 +103,8 @@
 
 
 def decode_kernel(win_hbm, count_ref, w_in_hbm, b_in_ref, g_one_ref, w_res_ref, b_res_ref, g_two_ref,
-                  block_hbm, branch_hbm, win_ref, w_in_ref, block_ref, branch_ref, w_buf, lat, lhs, edge, toep, pre,
-                  acts, masks, sems, load_sems, out_sems):
+                  block_hbm, branch_hbm, win_ref, w_in_ref, block_ref, branch_ref, w_buf, lat, taps_in, w_taps, pre,
+                  acts, operand, sums, masks, sems, load_sems, out_sems):
     c = b_in_ref.shape[0]
     load_w_in = pltpu.make_async_copy(w_in_hbm, w_in_ref, load_sems.at[0])
     load_win = pltpu.make_async_copy(win_hbm, win_ref, load_sems.at[1])
@@ -134,55 +134,44 @@
         masks[1, g] = jnp.where(first + g - 1 >= begin, 1.0, 0.0)
         masks[2, g] = jnp.where(first + g - 2 >= begin, 1.0, 0.0)
 
-    toep[...] = jnp.zeros_like(toep)
+    w_taps[...] = jnp.zeros_like(w_taps)
     load_w_in.wait()
-    for d in range(3):
-        for a in range(3):
-            j = 128 * (3 * d + a)
-            taps = w_in_ref[d, 48 * a:48 * a + 48, :].astype(BF16)
-            for x in range(8):
-                low, high = max(0, x - 1), min(7, x + 1)
-                skip = 16 * (low - x + 1)
-                toep[j + 16 * low:j + 16 * high + 16, c * x:c * x + c] = taps[skip:skip + 16 * (high - low + 1)]
-            toep[j + 112:j + 128, 8 * c:9 * c] = taps[:16]
-            toep[j:j + 16, 9 * c:10 * c] = taps[32:]
+    for j in range(9):
+        w_taps[64 * j:64 * j + 48, :] = w_in_ref[j // 3, 48 * (j % 3):48 * (j % 3) + 48, :].astype(BF16)
 
     lat[...] = jnp.zeros_like(lat)
     load_win.wait()
     for g in range(LT + 4):
         lat[stride * g + 3:stride * g + 3 + per_frame, :] = win_ref[per_frame * g:per_frame * (g + 1), :].astype(F32)
     row, lane = iota((per_frame, 128), 0) % 3, iota((per_frame, 128), 1)
-    from_right = (lane < 16) & (row != 2)
-    from_left = (lane >= 112) & (row != 0)
+    low_half = lane < 64
+    tiles = taps_in.shape[0]
     for g in range(LT + 2):
-        for d in range(3):
-            for a in range(3):
-                j = 128 * (3 * d + a)
-                base = stride * (g + 2 - d) + 3 * a
-                piece = lat[base:base + per_frame, :] * masks[d, g]
-                lhs[per_frame * g:per_frame * (g + 1), j:j + 128] = piece.astype(BF16)
-                beside = jnp.where(from_right, pltpu.roll(piece, per_frame - 1, 0),
-                                   jnp.where(from_left, pltpu.roll(piece, 1, 0), 0.0))
-                edge[per_frame * g:per_frame * (g + 1), j:j + 128] = beside.astype(BF16)
-
-    rows = per_frame * (LT + 2)
-    sides = jnp.dot(edge[...], toep[:, 8 * c:], preferred_element_type=F32)
-    for p in range(4):
-        out = jnp.dot(lhs[...], toep[:, 2 * c * p:2 * c * (p + 1)], preferred_element_type=F32)
-        even, odd = out[:, :c], out[:, c:]
-        if p == 0:
-            even = even + sides[:, :c]
-        if p == 3:
-            odd = odd + sides[:, c:]
-        for e, part in enumerate((even, odd)):
-            for q in range(c // 128):
-                pre[q, pl.ds(2 * p + e, rows, stride=8), :] = part[:, 128 * q:128 * q + 128]
+        pieces = []
+        for j in range(9):
+            base = stride * (g + 2 - j // 3) + 3 * (j % 3)
+            piece = lat[base:base + per_frame, :] * masks[j // 3, g]
+            left = jnp.where(lane >= 112, jnp.where(row != 0, pltpu.roll(piece, 1, 0), 0.0), piece)
+            right = jnp.where(lane < 16, jnp.where(row != 2, pltpu.roll(piece, per_frame - 1, 0), 0.0), piece)
+            pieces.append((left, piece, right))
+        for x in range(8):
+            moved = []
+            for j in range(9):
+                source = pieces[j][0 if x == 0 else 2 if x == 7 else 1]
+                amount = (64 * (j % 2) - 16 * (x - 1)) % 128
+                moved.append(pltpu.roll(source, amount, 1) if amount else source)
+            for t in range(tiles):
+                both = jnp.where(low_half, moved[2 * t], moved[2 * t + 1] if 2 * t + 1 < 9 else 0.0)
+                taps_in[t, pl.ds(g * frame + x, per_frame, stride=8), :] = both
+
+    windows = jnp.concatenate([taps_in[t].astype(BF16) for t in range(tiles)], axis=1)
+    pre[...] = jnp.dot(windows, w_taps[...], preferred_element_type=F32)
 
     column = iota((frame, c), 0) % WL
 
     def act_frame(g):
         at = slice(g * frame, (g + 1) * frame)
-        rounded = (jnp.concatenate([pre[q, at, :] for q in range(c // 128)], axis=1) + bias_one).astype(BF16)
+        rounded = (pre[at, :] + bias_one).astype(BF16)
         if g >= 2:
             block_ref[g - 2] = rounded
             block_out[g - 2].start()
@@ -198,11 +187,16 @@
     for copy in copies:
         copy.wait()
 
+    for f in range(LT):
+        for d in range(3):
+            values = acts[(f + 2 - d) * frame:(f + 3 - d) * frame, :]
+            if d > 0:
+                values = values * masks[d, f + 2].astype(BF16)
+            operand[f * frame:(f + 1) * frame, 3 * c * d:3 * c * (d + 1)] = values
+    sums[...] = jnp.dot(operand[...], w_buf[...], preferred_element_type=F32)
     blank = jnp.zeros((WL, c), F32)
     for f in range(LT):
-        taps = [acts[(f + 2 - d) * frame:(f + 3 - d) * frame, :] for d in range(3)]
-        taps = [taps[0]] + [taps[d] * masks[d, f + 2].astype(BF16) for d in (1, 2)]
-        out = jnp.dot(jnp.concatenate(taps, axis=1), w_buf[...], preferred_element_type=F32)
+        out = sums[f * frame:(f + 1) * frame, :]
         above = jnp.concatenate([blank, out[:-WL, :c]], axis=0)
         below = jnp.concatenate([out[WL:, 2 * c:], blank], axis=0)
         branch_ref[f] = silu_norm(above + out[:, c:2 * c] + below + bias_two, gain_two).astype(BF16)
@@ -264,11 +258,12 @@
             pltpu.VMEM((LT, frame, c), BF16),
             pltpu.VMEM((9 * c, 3 * c), BF16),
             pltpu.VMEM(((LT + 4) * (frame // 8 + 8), 128), F32),
-            pltpu.VMEM((act_rows // 8, 9 * 128), BF16),
-            pltpu.VMEM((act_rows // 8, 9 * 128), BF16),
-            pltpu.VMEM((9 * 128, 10 * c), BF16),
-            pltpu.VMEM((c // 128, act_rows, 128), F32),
+            pltpu.VMEM((5, act_rows, 128), F32),
+            pltpu.VMEM((5 * 128, c), BF16),
+            pltpu.VMEM((act_rows, c), F32),
             pltpu.VMEM((act_rows, 3 * c), BF16),
+            pltpu.VMEM((LT * frame, 9 * c), BF16),
+            pltpu.VMEM((LT * frame, 3 * c), F32),
             pltpu.SMEM((3, LT + 2), F32),
             pltpu.SemaphoreType.DMA((9,)),
             pltpu.SemaphoreType.DMA((2,)),

time: 43.3 us -> 45.7 us (1.055)
  Pallas kernels: 42.4 us -> 44.8 us
    pallas_call x1, Pallas kernels: 25.8 us -> 28.1 us  [local(): pl.pallas_call(decode_kernel, out_shape=[jax.ShapeDtypeStruct((LT, frame,...]
where the time goes in v5:
time: 45.7 us; the launch traced here: 45.6 us
  Pallas kernels  44.8 us (98%)
  between operations  0.8 us (2%)
    pallas_call x1, Pallas kernels, local(): pl.pallas_call(decode_kernel, out_shape=[jax.ShapeDtypeStruct((LT, frame,...  28.1 us
    pallas_call x1, Pallas kernels, local(): pl.pallas_call(functools.partial(regroup_kernel, n, br), out_shape=jax.Sh...  16.6 us

profile of v5, /device:TPU:0, one launch (start us, length us, event | category | flops | bytes accessed | tf_op | source)
XLA Modules:
  0.0 45.6 jit_solution(1039108560202925315)
XLA Ops:
  0.6 16.6 %shard_map.104.win_hbm = bf16[384,128]{1,0:T(8,128)(2,1)} custom-call(f32[192,128]{1,0:T(8,128)} %tiles_hbm.1, s32[1,192]{1,0:T(1,128)} %ids_hbm.1), custom_call_target="tpu_custom_call" | custom-call | tf_op jit(solution)/shard_map/pallas_call | solution.py:226
  17.3 28.1 %shard_map.105 = (bf16[4,384,384]{2,1,0:T(8,128)(2,1)}, bf16[4,384,384]{2,1,0:T(8,128)(2,1)}) custom-call(bf16[384,128]{1,0:T(8,128)(2,1)} %shard_map.104.win_hbm, s32[8]{0:T(128)} %count_ref.1, f32[3,144,384]{2,1,0:T(8,128)} %w_in_hbm.1, f32[384]{0:T(512)} %b_in_ref.1, f32[384]{0:T(512)} %g_one_ref.1, bf16[3,3456,384]{2,1,0:T(8,128)(2,1)} %w_res_ref.1, ...), custom_call_target="tpu_custom_call" | custom-call | flops 16000000000 | bytes 12000000 | tf_op jit(solution)/shard_map/pallas_call | solution.py:249
